TPU v7x, 256 devices: a whole 4x4x8 slice. The times are simulated.
256 devices in a mesh: section: 8 (over y, core), vocab: 8 (over z), dp: 4 (over x).
Axes of the slice: x: 4, y: 4, z: 8, core: 2. Of those that a mesh axis runs over, the one named last changes fastest.
Arguments:
- teacher_hidden: bfloat16 [640, 4096], P('dp', ('section', 'vocab')), as said below
- student_hidden: bfloat16 [640, 2048], P('dp', ('section', 'vocab')), as said below
- teacher_head: bfloat16 [4096, 65536], P('dp', ('section', 'vocab')), may hold values from -0.09375 to 0.09375
- student_head: bfloat16 [2048, 65536], P('dp', ('section', 'vocab')), may hold values from -0.125 to 0.125
- labels: int32 [640], P('dp'), may hold values from 0 to 65535
Outputs:
- loss: float32 [], replicated
- head_grad: float32 [2048, 65536], P('dp', ('section', 'vocab'))
- hidden_grad: bfloat16 [640, 2048], P('dp', ('section', 'vocab'))
Inputs may be any that keep to these rules, and one draw needn't show every extreme that they name: `teacher_hidden`: Real-valued activations. `student_hidden`: Real-valued activations.
All inputs are finite; a program needn't handle non-finite values.
Results may differ from a plain program's by a relative error of at most 0.012.
Values may be sent and summed in bfloat16 or wider, within the bound.
A program may use at most 64 MiB of HBM per device.

v0:
```python
import jax
import jax.numpy as jnp
from jax import lax
from jax.sharding import PartitionSpec as P

label_weight = 0.5


def per_device(teacher_hidden, student_hidden, teacher_head, student_head, labels):
    tokens = teacher_hidden.shape[0]
    block = teacher_head.shape[1]
    wide_t, wide_s = (
        lax.all_gather(teacher_hidden, ("section", "vocab"), axis=1, tiled=True),
        lax.all_gather(student_hidden, ("section", "vocab"), axis=1, tiled=True),
    )
    t_logits = jnp.dot(
        wide_t,
        lax.all_gather(teacher_head, "dp", axis=0, tiled=True),
        preferred_element_type=jnp.float32,
    )
    student_full = lax.all_gather(student_head, "dp", axis=0, tiled=True)
    s_logits = jnp.dot(wide_s, student_full, preferred_element_type=jnp.float32)
    offset = lax.axis_index(("section", "vocab")) * block
    column = offset + lax.broadcasted_iota(jnp.int32, (1, block), 1)
    target = (labels[:, None] == column).astype(jnp.float32)
    local_mt = jnp.max(t_logits, axis=1)
    local_ms = jnp.max(s_logits, axis=1)
    exp_t = jnp.exp(t_logits - local_mt[:, None])
    exp_s = jnp.exp(s_logits - local_ms[:, None])
    local_zt = jnp.sum(exp_t, axis=1)
    local_at = jnp.sum(exp_t * (t_logits - s_logits), axis=1)
    local_zs = jnp.sum(exp_s, axis=1)
    local_sy = jnp.sum(target * s_logits, axis=1)
    top_t, top_s = lax.pmax((local_mt, local_ms), ("section", "vocab"))
    shift_t = jnp.exp(local_mt - top_t)
    shift_s = jnp.exp(local_ms - top_s)
    total_t, cross, total_s, label_logit = lax.psum(
        (local_zt * shift_t, local_at * shift_t, local_zs * shift_s, local_sy), ("section", "vocab")
    )
    lse_t = top_t + jnp.log(total_t)
    lse_s = top_s + jnp.log(total_s)
    per_token = cross / total_t - lse_t + lse_s - label_weight * (label_logit - lse_s)
    loss = lax.psum(jnp.sum(per_token), "dp") / (tokens * lax.axis_size("dp"))
    probs_t = jnp.exp(t_logits - lse_t[:, None])
    probs_s = jnp.exp(s_logits - lse_s[:, None])
    logit_grad = ((1.0 + label_weight) * probs_s - probs_t - label_weight * target).astype(
        jnp.bfloat16
    )
    back_terms = lax.dot_general(
        logit_grad, student_full, (((1,), (1,)), ((), ())), preferred_element_type=jnp.float32
    )
    head_grad = lax.psum_scatter(
        lax.dot_general(
            wide_s, logit_grad, (((0,), (0,)), ((), ())), preferred_element_type=jnp.float32
        ).astype(jnp.bfloat16),
        "dp",
        scatter_dimension=0,
        tiled=True,
    ).astype(jnp.float32)
    hidden_grad = lax.psum_scatter(
        back_terms, ("section", "vocab"), scatter_dimension=1, tiled=True
    ).astype(jnp.bfloat16)
    return (loss, head_grad, hidden_grad)


def solution(mesh):
    in_specs = (
        P("dp", ("section", "vocab")),
        P("dp", ("section", "vocab")),
        P("dp", ("section", "vocab")),
        P("dp", ("section", "vocab")),
        P("dp"),
    )
    out_specs = (P(), P("dp", ("section", "vocab")), P("dp", ("section", "vocab")))
    return jax.shard_map(
        per_device, mesh=mesh, in_specs=in_specs, out_specs=out_specs, check_vma=False
    )
```

profile of v0, /device:TPU:4, one launch (start us, length us, event | category | flops | bytes accessed | tf_op | source)
XLA Modules:
  0.0 689.0 jit_solution(6850787520837899229)
XLA Ops:
  7.2 0.0 all-gather.8.cloned.1.call-start
  7.2 0.7 all-gather.8.cloned.1.call-update
  7.9 0.0 all-gather.4.cloned.1.call-start
  7.9 0.7 all-gather.4.cloned.1.call-update
  8.6 0.0 all-gather.6.cloned.1.call-start
  8.7 0.7 all-gather.6.cloned.1.call-update
  9.4 0.0 reduce-scatter.5.cloned.1.call-start
  9.4 52.6 %all_gather.14 = bf16[160,2048]{0,1:T(8,128)(2,1)S(1)} all-gather(bf16[160,32]{0,1:T(8,128)(2,1)} %param.6), channel_id=1, replica_groups=mesh['section'=8,'vocab'=8,'dp'=4] {'section','vocab'}, dimensions={1}, use_global_device_ids=true | all-gather | bytes 665600 | tf_op jit(solution)/shard_map/all_gather | solution.py:14
  62.1 0.6 all-gather.8.cloned.1.call-done
  62.6 3.2 fusion.7
  65.8 0.0 copy-start
  65.8 78.1 %all-gather.4.cloned.1.call-done = bf16[160,4096]{0,1:T(8,128)(2,1)} async-done(((bf16[160,64]{0,1:T(8,128)(2,1)}), bf16[160,4096]{0,1:T(8,128)(2,1)}) %all-gather.4.cloned.1.call-update) | async-done | bytes 1310736 | tf_op jit(solution)/shard_map/all_gather | solution.py:13
  143.9 84.9 %all-gather.6.cloned.1.call-done = bf16[4096,1024]{1,0:T(8,128)(2,1)} async-done(((bf16[1024,1024]{1,0:T(8,128)(2,1)}), bf16[4096,1024]{1,0:T(8,128)(2,1)}) %all-gather.6.cloned.1.call-update) | async-done | bytes 8388624 | tf_op jit(solution)/shard_map/all_gather | solution.py:18
  228.8 5.7 fusion.6
  234.5 129.0 %all-reduce.1 = (f32[160]{0:T(256)S(1)}, f32[160]{0:T(256)S(1)}) all-reduce(f32[160]{0:T(256)S(1)} %get-tuple-element.21, f32[160]{0:T(256)S(1)} %get-tuple-element.23), channel_id=1, replica_groups=mesh['section'=8,'vocab'=8,'dp'=4] {'section','vocab'}, use_global_device_ids=true, to_apply=%region_2.0 | all-reduce | flops 320 | bytes 2560 | tf_op jit(solution)/shard_map/pmax | solution.py:34
  363.5 0.0 copy-done
  363.5 0.5 multiply_reduce_fusion
  364.0 124.1 %all-reduce = (f32[160]{0:T(256)S(1)}, f32[160]{0:T(256)S(1)}, f32[160]{0:T(256)S(1)}, f32[160]{0:T(256)S(1)}) all-reduce(f32[160]{0:T(256)S(1)} %get-tuple-element.20, f32[160]{0:T(256)S(1)} %get-tuple-element.25, f32[160]{0:T(256)S(1)} %get-tuple-element.8, ...), channel_id=1, replica_groups=mesh['section'=8,'vocab'=8,'dp'=4] {'section','vocab'}, use_global_device_ids=true, to_apply=%region_5.0 | all-reduce | flops 640 | bytes 5120 | tf_op jit(solution)/shard_map/psum | solution.py:37
  488.1 0.6 subtract_reduce_fusion
  488.7 0.3 fusion.2
  489.1 4.8 fusion.8
  493.8 0.0 reduce-scatter.5.cloned.1.call-update
  493.9 0.0 reduce-scatter.3.cloned.1.call-start
  493.9 3.3 convert_bitcast_fusion
  497.2 0.0 reduce-scatter.3.cloned.1.call-update
  497.2 8.3 %psum.39 = f32[]{:T(128)} all-reduce(f32[]{:T(128)} %get-tuple-element.16), channel_id=1, replica_groups=mesh['section'=8,'vocab'=8,'dp'=4] {'dp'}, use_global_device_ids=true, to_apply=%region_13.0 | all-reduce | flops 1 | bytes 8 | tf_op jit(solution)/shard_map/psum | solution.py:43
  506.2 124.0 %reduce-scatter.5.cloned.1.call-done = f32[160,32]{0,1:T(8,128)} async-done(((f32[160,2048]{0,1:T(8,128)}), f32[160,32]{0,1:T(8,128)}) %reduce-scatter.5.cloned.1.call-update) | async-done | bytes 20496 | tf_op jit(solution)/shard_map/reduce_scatter | solution.py:60
  630.1 1.4 convert_element_type.20
  631.5 47.3 %reduce-scatter.3.cloned.1.call-done = bf16[512,1024]{0,1:T(8,128)(2,1)} async-done(((bf16[2048,1024]{0,1:T(8,128)(2,1)}), bf16[512,1024]{0,1:T(8,128)(2,1)}) %reduce-scatter.3.cloned.1.call-update) | async-done | bytes 1048592 | tf_op jit(solution)/shard_map/reduce_scatter | solution.py:52
  678.8 2.6 copy.8
  (2 shorter events, 0.0 us)
Async XLA Ops:
  7.2 55.5 %all-gather.8.cloned.1.call-start = ((), (), s32[]{:S(2)}) async-start(), calls=%async_computation.4 | async-start | bytes 5242880 | tf_op jit(solution)/shard_map/all_gather | solution.py:21
  7.9 136.0 %all-gather.4.cloned.1.call-start = ((), (), s32[]{:S(2)}) async-start(), calls=%async_computation.2 | async-start | bytes 2129920 | tf_op jit(solution)/shard_map/all_gather | solution.py:13
  8.6 220.2 %all-gather.6.cloned.1.call-start = ((), (), s32[]{:S(2)}) async-start(), calls=%async_computation.3 | async-start | bytes 10485760 | tf_op jit(solution)/shard_map/all_gather | solution.py:18
  9.4 620.7 %reduce-scatter.5.cloned.1.call-start = ((), (), s32[]{:S(2)}) async-start(), calls=%async_computation.6 | async-start | bytes 2129920 | tf_op jit(solution)/shard_map/reduce_scatter | solution.py:60
  65.8 297.7 %copy-start = (s32[160]{0:T(256)S(1)}, s32[160]{0:T(256)}, u32[]{:S(2)}) copy-start(s32[160]{0:T(256)} %param.9) | copy-start | bytes 1924
  493.9 184.9 %reduce-scatter.3.cloned.1.call-start = ((), (), s32[]{:S(2)}) async-start(), calls=%async_computation.5 | async-start | bytes 5242880 | tf_op jit(solution)/shard_map/reduce_scatter | solution.py:52
Sparse Core Ops, SparseCore 0:
  9.8 52.7 all-gather.7
  65.4 78.4 all-gather.3
  145.8 83.0 all-gather.5
  494.0 136.0 reduce-scatter.4
  632.7 46.0 reduce-scatter.2
where the time goes:
time: 692 us; the launch traced here: 689 us
  waiting for transfers between devices  337 us (49%)
  blocking collectives  314 us (45%)
  matrix products  16.9 us (2%)
  between operations  15.6 us (2%)
    pmax x1, blocking collectives, per_device(): top_t, top_s = lax.pmax((local_mt, local_ms), ('section', 'vocab'))  129 us
    psum x1, blocking collectives, per_device(): lax.psum((local_zt * shift_t, local_at * shift_t, local_zs * shift_s, loc...  124 us
    reduce_scatter x1, waiting for transfers between devices, per_device(): lax.psum_scatter(back_terms, ('section', 'vocab'), scatter_dimension=1, t...  124 us
    all_gather x1, waiting for transfers between devices, per_device(): lax.all_gather(teacher_head, 'dp', axis=0, tiled=True)  84.9 us
    all_gather x1, waiting for transfers between devices, per_device(): lax.all_gather(teacher_hidden, ('section', 'vocab'), axis=1, tiled=True)  78.1 us
    all_gather x1, blocking collectives, per_device(): lax.all_gather(student_hidden, ('section', 'vocab'), axis=1, tiled=True)  52.6 us
    reduce_scatter x1, waiting for transfers between devices, per_device(): lax.psum_scatter(lax.dot_general(wide_s, logit_grad, (((0,), (0,)), ((),...  47.3 us
  transfers between devices with their start and end apart: 5, of which 5 were waited for; matrix products, arithmetic and copies ran while one was open for 1% of the time, Pallas kernels for 0%

commit v1 on v0

v1 whole, which is shorter than its diff:
```python
import functools
import jax
import jax.numpy as jnp
from jax import lax
from jax.experimental import pallas as pl
from jax.experimental.pallas import tpu as pltpu
from jax.sharding import PartitionSpec as P

label_weight = 0.5
MESH = pl.DeviceIdType.MESH
F32, BF16, I32, I16 = jnp.float32, jnp.bfloat16, jnp.int32, jnp.int16
TOP = 14.99


def mm(a, b):
    return jnp.dot(a, b, preferred_element_type=F32)


def mm_nt(a, b):
    return lax.dot_general(a, b, (((1,), (1,)), ((), ())), preferred_element_type=F32)


def iota(shape, dim):
    return lax.broadcasted_iota(I32, shape, dim)


def ones_where(mask):
    return jnp.where(mask, 1.0, 0.0).astype(BF16)


def kernel(
    th, sh, wt_hbm, ws_hbm, lab,
    loss_out, hg, hid_out,
    wt, ws, packed, hslot, hid, hst, part, own_t, own_s,
    qsend, qrecv, grad, stat, stat_in, stat_mid, loss_in, cols_a, cols_b,
    hown, cbuf, crcv, zbuf, zrcv, ybuf, yrcv, fin, frcv,
    w_sem, h1_s, h1_r, zf_s, zf_r, zb_s, zb_r, cc_s, cc_r,
    q_s, q_r, st_s, st_r, sm_s, sm_r, lo_s, lo_r, g_s, g_r,
    c_s, c_r, z_s, z_r, y_s, y_r, f_s, f_r,
):
    tb = th.shape[0]
    half = tb // 2
    vb = wt.shape[1]
    ks = 128
    s = lax.axis_index("section")
    z = lax.axis_index("vocab")
    x = lax.axis_index("dp")
    y, c = lax.div(s, 2), lax.rem(s, 2)
    g4, j4 = lax.div(z, 4) * 4, lax.rem(z, 4)
    right, left, opp = lax.rem(x + 1, 4), lax.rem(x + 3, 4), lax.rem(x + 2, 4)
    mine = jnp.logical_and(x == y, j4 == x)
    pending = []

    def dev(section=s, vocab=z, dp=x):
        return {"section": section, "vocab": vocab, "dp": dp}

    def remote(src, dst, ssem, rsem, to):
        return pltpu.make_async_remote_copy(
            src_ref=src, dst_ref=dst, send_sem=ssem, recv_sem=rsem,
            device_id=to, device_id_type=MESH,
        )

    def send(src, dst, ssem, rsem, to):
        copy = remote(src, dst, ssem, rsem, to)
        copy.start()
        pending.append((None, copy))

    def send_if(cond, src, dst, ssem, rsem, to):
        copy = remote(src, dst, ssem, rsem, to)
        pl.when(cond)(copy.start)
        pending.append((cond, copy))

    def arrived(dst, ssem, rsem):
        remote(dst, dst, ssem, rsem, dev(dp=right)).wait_recv()

    load_t = pltpu.make_async_copy(wt_hbm, wt, w_sem.at[0])
    load_s = pltpu.make_async_copy(ws_hbm, ws, w_sem.at[1])
    load_t.start()
    load_s.start()

    barrier = pltpu.get_barrier_semaphore()

    def greet(to):
        pl.semaphore_signal(barrier, inc=1, device_id=to, device_id_type=MESH)

    for k in range(1, 4):
        greet(dev(dp=lax.rem(x + k, 4)))
    for k in range(1, 8):
        greet(dev(vocab=lax.rem(z + k, 8)))
        greet(dev(section=lax.rem(s + k, 8)))
    for k in range(4):
        to = dev(section=2 * k + c, vocab=g4 + x, dp=y)
        pl.when(jnp.logical_not(jnp.logical_and(mine, y == k)))(functools.partial(greet, to))
        frm = dev(section=2 * x + c, vocab=g4 + k, dp=j4)
        pl.when(jnp.logical_not(jnp.logical_and(mine, j4 == k)))(functools.partial(greet, frm))

    packed[...] = (
        mm(th[...], ones_where(iota((64, 128), 0) == iota((64, 128), 1)))
        + mm(sh[...], ones_where(iota((32, 128), 0) + 64 == iota((32, 128), 1)))
    ).astype(BF16)
    pl.semaphore_wait(barrier, 25 - 2 * mine.astype(I32))

    for k in range(4):
        send_if(
            jnp.logical_not(jnp.logical_and(mine, y == k)),
            packed, hslot.at[j4], h1_s.at[k], h1_r.at[j4],
            dev(section=2 * k + c, vocab=g4 + x, dp=y),
        )

    @pl.when(mine)
    def _():
        hslot[j4] = packed[...]

    cols_b[...] = jnp.zeros_like(cols_b)
    cols_b[0:1, 0:tb] = lab[...].astype(F32)
    lab_cols = cols_b[...].T
    cols_a[...] = lab_cols
    stat[...] = jnp.ones_like(stat)

    unit = None
    for k in range(4):
        @pl.when(jnp.logical_not(jnp.logical_and(mine, j4 == k)))
        def _(k=k):
            arrived(hslot.at[k], h1_s.at[k], h1_r.at[k])

    for k in range(4):
        rows, lanes = iota((128, 384), 0), iota((128, 384), 1)
        place = jnp.where(rows < 64, rows + 64 * k, rows - 64 + 256 + 32 * k)
        pick = ones_where(jnp.logical_and(lanes == place, rows < 96))
        term = mm(hslot[k], pick)
        unit = term if unit is None else unit + term
    hid[c, z] = unit.astype(BF16)

    sgn = 1 - 2 * c
    ahead, behind = lax.rem(z + sgn + 8, 8), lax.rem(z - sgn + 8, 8)
    other = dev(section=s + sgn)

    def rows_of(h):
        return pl.ds(h * half, half)

    def block(k):
        return lax.rem(z + k * sgn + 16, 8)

    def to_ahead(k, h):
        b = block(1 - k)
        ref = hid.at[c, b, rows_of(h)]
        send(ref, ref, zf_s.at[2 * k - 2 + h], zf_r.at[2 * k - 2 + h], dev(vocab=ahead))

    def to_behind(k, h):
        b = block(k - 1)
        ref = hid.at[c, b, rows_of(h)]
        send(ref, ref, zb_s.at[2 * k - 2 + h], zb_r.at[2 * k - 2 + h], dev(vocab=behind))

    def to_other(b, h):
        ref = hid.at[c, b, rows_of(h)]
        send(ref, ref, cc_s.at[2 * b + h], cc_r.at[2 * b + h], other)

    for h in range(2):
        to_ahead(1, h)
        to_behind(1, h)
    for h in range(2):
        to_other(z, h)
    for k in range(1, 5):
        for h in range(2):
            b = block(-k)
            arrived(hid.at[c, b, rows_of(h)], zf_s.at[2 * k - 2 + h], zf_r.at[2 * k - 2 + h])
            if k < 4:
                to_ahead(k + 1, h)
            to_other(b, h)
            if k < 4:
                b = block(k)
                arrived(hid.at[c, b, rows_of(h)], zb_s.at[2 * k - 2 + h], zb_r.at[2 * k - 2 + h])
                if k < 3:
                    to_behind(k + 1, h)
                to_other(b, h)
    load_t.wait()
    load_s.wait()
    for b in range(8):
        for h in range(2):
            arrived(hid.at[1 - c, b, rows_of(h)], cc_s.at[2 * b + h], cc_r.at[2 * b + h])

    def logits_t(xp, out):
        def body(n, carry):
            cols = pl.ds(pl.multiple_of(n * 256, 256), 256)
            total = None
            for u in range(4):
                term = mm(hid[u // 2, 4 * (u % 2) + xp, :, 0:256], wt[u * 256:(u + 1) * 256, cols])
                total = term if total is None else total + term
            out[:, cols] = total
            return carry
        lax.fori_loop(0, vb // 256, body, 0)

    def logits_s(xp, out):
        def body(n, carry):
            cols = pl.ds(pl.multiple_of(n * 256, 256), 256)
            total = None
            for u in range(4):
                term = mm(hid[u // 2, 4 * (u % 2) + xp, :, 256:384], ws[u * ks:(u + 1) * ks, cols])
                total = term if total is None else total + term
            out[:, cols] = total
            return carry
        lax.fori_loop(0, vb // 256, body, 0)

    def decode(slot, rows):
        step = jnp.exp2(qrecv[slot, rows, vb:vb + 128].astype(F32) * 0.25 - TOP)
        return jnp.concatenate(
            [qrecv[slot, rows, i:i + 128].astype(F32) * step for i in range(0, vb, 128)], axis=1
        )

    def encode(slot, src, add=None):
        def body(r, carry):
            rows = pl.ds(pl.multiple_of(r * 16, 16), 16)
            v = src[rows, :]
            if add is not None:
                v = v + decode(add, rows)
            top = jnp.maximum(jnp.max(jnp.abs(v), axis=1, keepdims=True), 1e-30)
            level = jnp.broadcast_to(jnp.ceil(jnp.log2(top) * 4.0), (16, 128))
            scale = jnp.exp2(TOP - level * 0.25)
            for i in range(0, vb, 128):
                q = jnp.round(v[:, i:i + 128] * scale).astype(I32)
                qsend[slot, rows, i:i + 128] = q.astype(I16)
            qsend[slot, rows, vb:vb + 128] = level.astype(I32).astype(I16)
            return carry
        lax.fori_loop(0, tb // 16, body, 0)

    def ship(slot, dp):
        send(qsend.at[slot], qrecv.at[slot], q_s.at[slot], q_r.at[slot], dev(dp=dp))

    def landed(slot):
        arrived(qrecv.at[slot], q_s.at[slot], q_r.at[slot])

    logits_t(opp, part)
    encode(0, part)
    ship(0, right)
    logits_s(opp, part)
    encode(3, part)
    ship(3, left)
    logits_s(right, part)
    encode(1, part)
    ship(1, right)
    logits_t(left, part)
    encode(4, part)
    ship(4, left)
    logits_t(right, own_t)
    logits_s(left, own_s)
    landed(0)
    encode(2, own_t, add=0)
    ship(2, right)
    landed(3)
    encode(5, own_s, add=3)
    ship(5, left)
    logits_t(x, own_t)
    logits_s(x, own_s)

    eye = ones_where(iota((128, 128), 0) == iota((128, 128), 1))
    for u in range(4):
        def turn(xp, carry, u=u):
            flat = mm_nt(eye, hid[u // 2, 4 * (u % 2) + xp, :, 256:384])
            hst[xp, u * 128:(u + 1) * 128, :] = flat.astype(BF16)
            return carry
        lax.fori_loop(0, 4, turn, 0)

    landed(1)
    landed(4)
    landed(2)
    landed(5)

    offset = (s * 8 + z) * vb

    def collect(r, carry):
        rows = pl.ds(pl.multiple_of(r * 16, 16), 16)
        lt = own_t[rows, :] + decode(4, rows) + decode(2, rows)
        ls = own_s[rows, :] + decode(1, rows) + decode(5, rows)
        own_t[rows, :] = lt
        own_s[rows, :] = ls
        mt = jnp.max(lt, axis=1, keepdims=True)
        ms = jnp.max(ls, axis=1, keepdims=True)
        et = jnp.exp(lt - mt)
        es = jnp.exp(ls - ms)
        column = offset + iota((16, vb), 1)
        hit = column == cols_a[rows, 0:1].astype(I32)
        values = (
            mt,
            jnp.sum(et, axis=1, keepdims=True),
            jnp.sum(et * (lt - ls), axis=1, keepdims=True),
            ms,
            jnp.sum(es, axis=1, keepdims=True),
            jnp.sum(jnp.where(hit, ls, 0.0), axis=1, keepdims=True),
        )
        lane = iota((16, 128), 1)
        out = jnp.ones((16, 128), F32)
        for i, value in enumerate(values):
            out = jnp.where(lane == i, value, out)
        stat[rows, :] = out
        return carry

    lax.fori_loop(0, tb // 16, collect, 0)

    def merge(ref):
        tops_t = [ref[i, 0:1, :] for i in range(8)]
        tops_s = [ref[i, 3:4, :] for i in range(8)]
        mt = functools.reduce(jnp.maximum, tops_t)
        ms = functools.reduce(jnp.maximum, tops_s)
        zt = at = zs = sy = 0.0
        for i in range(8):
            wt_i = jnp.exp(tops_t[i] - mt)
            ws_i = jnp.exp(tops_s[i] - ms)
            zt = zt + ref[i, 1:2, :] * wt_i
            at = at + ref[i, 2:3, :] * wt_i
            zs = zs + ref[i, 4:5, :] * ws_i
            sy = sy + ref[i, 5:6, :]
        return mt, zt, at, ms, zs, sy

    turned = stat[...].T
    stat_in[z] = turned[0:8, :]
    for k in range(1, 8):
        send(stat_in.at[z], stat_in.at[z], st_s.at[k], st_r.at[z], dev(vocab=lax.rem(z + k, 8)))
    for k in range(1, 8):
        frm = lax.rem(z + k, 8)
        arrived(stat_in.at[frm], st_s.at[k], st_r.at[frm])
    pieces = merge(stat_in)
    for i, piece in enumerate(pieces):
        stat_mid[s, i:i + 1, :] = piece
    for k in range(1, 8):
        send(stat_mid.at[s], stat_mid.at[s], sm_s.at[k], sm_r.at[s], dev(section=lax.rem(s + k, 8)))
    for k in range(1, 8):
        frm = lax.rem(s + k, 8)
        arrived(stat_mid.at[frm], sm_s.at[k], sm_r.at[frm])
    mt, zt, at, ms, zs, sy = merge(stat_mid)
    lse_t = mt + jnp.log(zt)
    lse_s = ms + jnp.log(zs)
    per_token = at / zt - lse_t + lse_s - label_weight * (sy - lse_s)
    per_token = jnp.where(iota((1, 256), 1) < tb, per_token, 0.0)
    cols_b[0:1, :] = lse_t
    cols_b[1:2, :] = lse_s
    turned = cols_b[...].T
    stat[...] = turned

    def finish(r, carry):
        rows = pl.ds(pl.multiple_of(r * 16, 16), 16)
        column = offset + iota((16, vb), 1)
        hit = column == cols_a[rows, 0:1].astype(I32)
        pt = jnp.exp(own_t[rows, :] - stat[rows, 0:1])
        ps = jnp.exp(own_s[rows, :] - stat[rows, 1:2])
        value = (1.0 + label_weight) * ps - pt - jnp.where(hit, label_weight, 0.0)
        grad[x, rows, :] = value.astype(BF16)
        return carry

    def gsend(owner, h, i, dp):
        ref = grad.at[owner, rows_of(h)]
        send(ref, ref, g_s.at[i], g_r.at[i], dev(dp=dp))

    def gwait(owner, h, i):
        arrived(grad.at[owner, rows_of(h)], g_s.at[i], g_r.at[i])

    lax.fori_loop(0, half // 16, finish, 0)
    gsend(x, 0, 0, right)
    gsend(x, 0, 3, left)
    lax.fori_loop(half // 16, tb // 16, finish, 0)
    gsend(x, 1, 2, left)
    gsend(x, 1, 1, right)
    loss_in[x] = jnp.broadcast_to(jnp.sum(per_token, axis=1, keepdims=True), (8, 128))
    for k in range(1, 4):
        send(loss_in.at[x], loss_in.at[x], lo_s.at[k], lo_r.at[x], dev(dp=lax.rem(x + k, 4)))

    def hidden_terms(xp):
        for g in range(2):
            u = (1 - c) * 2 + g
            rows = pl.ds(pl.multiple_of(u * ks, ks), ks)
            cbuf[xp, g] = mm_nt(grad[xp], ws[rows, :]).astype(BF16)
        send(cbuf.at[xp], crcv.at[xp], c_s.at[xp], c_r.at[xp], other)
        for g in range(2):
            u = c * 2 + g
            rows = pl.ds(pl.multiple_of(u * ks, ks), ks)
            hown[xp, g] = mm_nt(grad[xp], ws[rows, :])

    def head_terms(xp, first):
        def body(n, carry):
            cols = pl.ds(pl.multiple_of(n * 256, 256), 256)
            term = mm(hst[xp], grad[xp, :, cols])
            hg[:, cols] = term if first else hg[:, cols] + term
            return carry
        lax.fori_loop(0, vb // 256, body, 0)

    def spread(xp):
        arrived(crcv.at[xp], c_s.at[xp], c_r.at[xp])
        for g in range(2):
            total = hown[xp, g] + crcv[xp, g].astype(F32)
            hown[xp, g] = total
            zbuf[xp, g] = total.astype(BF16)
            to = 4 * g + xp
            send_if(to != z, zbuf.at[xp, g], zrcv.at[z], z_s.at[2 * xp + g], z_r.at[z], dev(vocab=to))

    hidden_terms(x)
    head_terms(x, True)
    spread(x)
    gwait(left, 0, 0)
    gsend(left, 0, 4, right)
    gwait(right, 1, 2)
    gsend(right, 1, 5, left)
    gwait(left, 1, 1)
    hidden_terms(left)
    head_terms(left, False)
    spread(left)
    gwait(right, 0, 3)
    hidden_terms(right)
    head_terms(right, False)
    spread(right)
    gwait(opp, 0, 4)
    gwait(opp, 1, 5)
    hidden_terms(opp)
    head_terms(opp, False)
    spread(opp)

    total = hown[j4, lax.div(z, 4)]
    for k in range(1, 8):
        frm = lax.rem(z + k, 8)
        arrived(zrcv.at[frm], z_s.at[k], z_r.at[frm])
        total = total + zrcv[frm].astype(F32)
    ybuf[...] = total.astype(BF16)
    send_if(x != y, ybuf, yrcv.at[y], y_s, y_r.at[y], dev(section=2 * x + c))
    hown[j4, lax.div(z, 4)] = total

    @pl.when(x == y)
    def _():
        whole = hown[j4, lax.div(z, 4)]
        for k in range(1, 4):
            frm = lax.rem(y + k, 4)
            arrived(yrcv.at[frm], y_s, y_r.at[frm])
            whole = whole + yrcv[frm].astype(F32)
        fin[...] = whole.astype(BF16)

    for k in range(4):
        there = jnp.logical_and(j4 == x, j4 == k)
        send_if(
            jnp.logical_and(x == y, jnp.logical_not(there)),
            fin, frcv, f_s.at[k], f_r, dev(vocab=g4 + k, dp=j4),
        )

    @pl.when(mine)
    def _():
        frcv[...] = fin[...]

    @pl.when(jnp.logical_not(mine))
    def _():
        arrived(frcv, f_s.at[0], f_r)

    pick = ones_where(iota((128, 32), 0) == iota((128, 32), 1) + 32 * j4)
    hid_out[...] = mm(frcv[...], pick).astype(BF16)

    loss = loss_in[x, 0:1, 0:1]
    for k in range(1, 4):
        frm = lax.rem(x + k, 4)
        arrived(loss_in.at[frm], lo_s.at[k], lo_r.at[frm])
    loss = loss_in[0, 0:1, 0:1] + loss_in[1, 0:1, 0:1] + loss_in[2, 0:1, 0:1] + loss_in[3, 0:1, 0:1]
    loss_out[0, 0] = jnp.sum(loss) / (4.0 * tb)

    for cond, copy in pending:
        if cond is None:
            copy.wait_send()
        else:
            pl.when(cond)(copy.wait_send)


def per_device(teacher_hidden, student_hidden, teacher_head, student_head, labels):
    tb = teacher_hidden.shape[0]
    kt, vb = teacher_head.shape
    ks = student_head.shape[0]
    dma, vmem = pltpu.SemaphoreType.DMA, pltpu.VMEM
    loss, head_grad, hidden_grad = pl.pallas_call(
        kernel,
        out_shape=(
            jax.ShapeDtypeStruct((1, 1), F32),
            jax.ShapeDtypeStruct((ks, vb), F32),
            jax.ShapeDtypeStruct((tb, 32), BF16),
        ),
        in_specs=[
            pl.BlockSpec(memory_space=pltpu.VMEM),
            pl.BlockSpec(memory_space=pltpu.VMEM),
            pl.BlockSpec(memory_space=pl.ANY),
            pl.BlockSpec(memory_space=pl.ANY),
            pl.BlockSpec(memory_space=pltpu.VMEM),
        ],
        out_specs=(
            pl.BlockSpec(memory_space=pltpu.SMEM),
            pl.BlockSpec(memory_space=pltpu.VMEM),
            pl.BlockSpec(memory_space=pltpu.VMEM),
        ),
        scratch_shapes=[
            vmem((kt, vb), BF16),
            vmem((ks, vb), BF16),
            vmem((tb, 128), BF16),
            vmem((4, tb, 128), BF16),
            vmem((2, 8, tb, 384), BF16),
            vmem((4, ks, tb), BF16),
            vmem((tb, vb), F32),
            vmem((tb, vb), F32),
            vmem((tb, vb), F32),
            vmem((6, tb, vb + 128), I16),
            vmem((6, tb, vb + 128), I16),
            vmem((4, tb, vb), BF16),
            vmem((256, 128), F32),
            vmem((8, 8, 256), F32),
            vmem((8, 8, 256), F32),
            vmem((4, 8, 128), F32),
            vmem((256, 128), F32),
            vmem((128, 256), F32),
            vmem((4, 2, tb, 128), F32),
            vmem((4, 2, tb, 128), BF16),
            vmem((4, 2, tb, 128), BF16),
            vmem((4, 2, tb, 128), BF16),
            vmem((8, tb, 128), BF16),
            vmem((tb, 128), BF16),
            vmem((4, tb, 128), BF16),
            vmem((tb, 128), BF16),
            vmem((tb, 128), BF16),
            dma((2,)), dma((4,)), dma((4,)),
            dma((8,)), dma((8,)), dma((6,)), dma((6,)), dma((16,)), dma((16,)),
            dma((6,)), dma((6,)), dma((8,)), dma((8,)), dma((8,)), dma((8,)),
            dma((4,)), dma((4,)), dma((6,)), dma((6,)),
            dma((4,)), dma((4,)), dma((8,)), dma((8,)),
            dma, dma((4,)), dma((4,)), dma,
        ],
        compiler_params=pltpu.CompilerParams(
            collective_id=0, has_side_effects=True, vmem_limit_bytes=48 * 1024 * 1024
        ),
    )(teacher_hidden, student_hidden, teacher_head, student_head, labels.reshape(1, tb))
    return (loss.reshape(()), head_grad, hidden_grad)


def solution(mesh):
    spec = P("dp", ("section", "vocab"))
    return jax.shard_map(
        per_device,
        mesh=mesh,
        in_specs=(spec, spec, spec, spec, P("dp")),
        out_specs=(P(), spec, spec),
        check_vma=False,
    )
```

time: 692 us -> 126 us (0.18)
  waiting for transfers between devices: 337 us -> 0 us
  blocking collectives: 314 us -> 0 us
  Pallas kernels: 0 us -> 116 us
  matrix products: 16.9 us -> 0 us
  between operations: 15.6 us -> 2.39 us
    reduce_scatter x2 -> x0, waiting for transfers between devices: 171 us -> none  [the longest x1 124 us: per_device(): lax.psum_scatter(back_terms, ('section', 'vocab'), scatter_dimension=1, t...]
    all_gather x3 -> x0, waiting for transfers between devices: 164 us -> none  [the longest x1 84.9 us: per_device(): lax.all_gather(teacher_head, 'dp', axis=0, tiled=True)]
    psum x2 -> x0, blocking collectives: 132 us -> none  [the longest x1 124 us: per_device(): lax.psum((local_zt * shift_t, local_at * shift_t, local_zs * shift_s, loc...]
    pmax x1 -> x0, blocking collectives: 129 us -> none  [per_device(): top_t, top_s = lax.pmax((local_mt, local_ms), ('section', 'vocab'))]
    pallas_call x0 -> x1, Pallas kernels: none -> 116 us  [per_device(): pl.pallas_call(kernel, out_shape=(jax.ShapeDtypeStruct((1, 1), F32), jax....]
    all_gather x1 -> x0, blocking collectives: 52.6 us -> none  [per_device(): lax.all_gather(student_hidden, ('section', 'vocab'), axis=1, tiled=True)]
    dot_general x4 -> x0, matrix products: 16.9 us -> none  [the longest x1 5.67 us: per_device(): jnp.dot(wide_t, lax.all_gather(teacher_head, 'dp', axis=0, tiled=True), p...]
  transfers between devices with their start and end apart: 5 -> 0, of which waited for: 5 -> 0; matrix products, arithmetic and copies ran while one was open for 1% -> 0% of each run, Pallas kernels for 0% -> 0%
where the time goes in v1:
time: 126 us; the launch traced here: 125 us
  Pallas kernels  116 us (92%)
  local copies, waits for them, and re-layouts  7.21 us (6%)
  between operations  2.39 us (2%)
    pallas_call x1, Pallas kernels, per_device(): pl.pallas_call(kernel, out_shape=(jax.ShapeDtypeStruct((1, 1), F32), jax....  116 us
    unnamed x10, local copies, waits for them, and re-layouts  7.21 us

profile of v1, /device:TPU:4, one launch (start us, length us, event | category | flops | bytes accessed | tf_op | source)
XLA Modules:
  0.0 125.3 jit_solution(15435232313302421526)
XLA Ops:
  0.6 0.9 copy.8.th
  1.5 0.8 copy.9.sh
  2.3 0.0 copy-start
  2.3 1.6 %copy-done = bf16[1024,1024]{1,0:T(8,128)(2,1)S(1)} copy-done((bf16[1024,1024]{1,0:T(8,128)(2,1)S(1)}, bf16[1024,1024]{1,0:T(8,128)(2,1)}, u32[]{:S(2)}) %copy-start) | copy-done | bytes 2097176
  3.9 0.0 copy-start.1
  3.9 1.2 copy-done.1
  5.2 0.0 copy-start.2
  5.2 0.7 copy-done.2
  5.8 115.7 %shard_map.76 = (f32[1,1]{1,0:T(1,128)}, f32[512,1024]{1,0:T(8,128)S(1)}, bf16[160,32]{1,0:T(8,128)(2,1)S(1)}) custom-call(bf16[160,64]{1,0:T(8,128)(2,1)S(1)} %copy.8.th, bf16[160,32]{1,0:T(8,128)(2,1)S(1)} %copy.9.sh, bf16[1024,1024]{1,0:T(8,128)(2,1)S(1)} %copy-done, bf16[512,1024]{1,0:T(8,128)(2,1)S(1)} %copy-done.1, s32[1,160]{1,0:T(1,128)S(1)} %bitcast.2), custom_call_target="tpu_custom_call" | custom-call | tf_op jit(solution)/shard_map/pallas_call | solution.py:470
  121.5 0.7 copy.10
  122.8 1.3 %copy.14 = f32[512,1024]{1,0:T(8,128)} copy(f32[512,1024]{1,0:T(8,128)S(1)} %get-tuple-element.16) | data formatting | bytes 4194304
Async XLA Ops:
  2.3 1.6 %copy-start = (bf16[1024,1024]{1,0:T(8,128)(2,1)S(1)}, bf16[1024,1024]{1,0:T(8,128)(2,1)}, u32[]{:S(2)}) copy-start(bf16[1024,1024]{1,0:T(8,128)(2,1)} %wt_hbm.1) | copy-start | bytes 6291460
  3.9 1.2 copy-start.1
  5.2 0.7 copy-start.2

commit v2 on v0

v2 whole, which is shorter than its diff:
```python
import functools
import jax
import jax.numpy as jnp
from jax import lax
from jax.experimental import pallas as pl
from jax.experimental.pallas import tpu as pltpu
from jax.sharding import PartitionSpec as P

label_weight = 0.5
MESH = pl.DeviceIdType.MESH
F32, BF16, I32, I16 = jnp.float32, jnp.bfloat16, jnp.int32, jnp.int16
TOP = 14.99
PARTS = (48, 64, 48)
ORDER = (
    "F2", "F1", "I", "Z2", "F0", "Z1", "Y2", "Y1", "W2", "Z0", "L2", "W1", "Y0", "U2",
    "O2", "L1", "T2", "W0", "O1", "L0", "U1", "T1", "S2", "O0", "S1", "G2", "T0", "G1",
    "U0", "S0", "B2", "G0", "P2", "B1", "P1", "B0", "P0", "N1", "X", "N2", "H", "X2",
    "N0", "E",
)


def mm(a, b):
    return jnp.dot(a, b, preferred_element_type=F32)


def mm_nt(a, b):
    return lax.dot_general(a, b, (((1,), (1,)), ((), ())), preferred_element_type=F32)


def iota(shape, dim):
    return lax.broadcasted_iota(I32, shape, dim)


def ones_where(mask):
    return jnp.where(mask, 1.0, 0.0).astype(BF16)


def buffers(tb, kt, ks, vb):
    dma, vmem = pltpu.SemaphoreType.DMA, pltpu.VMEM

    def each(make):
        return [make(n) for n in PARTS]

    return {
        "wt": vmem((kt, vb), BF16),
        "ws": vmem((ks, vb), BF16),
        "lab": vmem((1, tb), I32),
        "turned": vmem((128, tb), BF16),
        "packed": vmem((tb, 128), BF16),
        "wide": vmem((128, 256), F32),
        "lab_col": vmem((256, 128), F32),
        "raw": each(lambda n: vmem((8, n, 128), BF16)),
        "hid": each(lambda n: vmem((2, 4 * n, 768), BF16)),
        "hst": each(lambda n: vmem((ks, 4 * n), BF16)),
        "part_t": each(lambda n: vmem((4 * n, vb), F32)),
        "part_s": each(lambda n: vmem((4 * n, vb), F32)),
        "qsend": each(lambda n: vmem((6, n, vb + 128), I16)),
        "qrecv": each(lambda n: vmem((6, n, vb + 128), I16)),
        "level": each(lambda n: vmem((2, n, 128), F32)),
        "stat": each(lambda n: vmem((128, 128), F32)),
        "lse": each(lambda n: vmem((128, 128), F32)),
        "stat_z": each(lambda n: vmem((8, 8, 128), F32)),
        "stat_s": each(lambda n: vmem((8, 8, 128), F32)),
        "grad": each(lambda n: vmem((4 * n, vb), BF16)),
        "hown": each(lambda n: vmem((256, 4 * n), F32)),
        "csend": each(lambda n: vmem((256, 4 * n), BF16)),
        "crecv": each(lambda n: vmem((256, 4 * n), BF16)),
        "zsend": each(lambda n: vmem((256, 4 * n), BF16)),
        "zrecv": each(lambda n: vmem((8, 32, 4 * n), BF16)),
        "fsend": each(lambda n: vmem((32, 4 * n), BF16)),
        "frecv": each(lambda n: vmem((4, 32, 4 * n), BF16)),
        "loss": vmem((4, 8, 128), F32),
        "in_sem": dma((5,)),
        "h_s": each(lambda n: dma),
        "h_r": each(lambda n: dma),
        "r_s": each(lambda n: dma((8,))),
        "r_r": each(lambda n: dma((8,))),
        "u_s": each(lambda n: dma((4,))),
        "u_r": each(lambda n: dma((4,))),
        "w_s": each(lambda n: dma((4,))),
        "w_r": each(lambda n: dma((4,))),
        "q_s": each(lambda n: dma((6,))),
        "q_r": each(lambda n: dma((6,))),
        "sz_s": each(lambda n: dma((8,))),
        "sz_r": each(lambda n: dma((8,))),
        "ss_s": each(lambda n: dma((8,))),
        "ss_r": each(lambda n: dma((8,))),
        "g_s": each(lambda n: dma((4,))),
        "g_r": each(lambda n: dma((4,))),
        "c_s": each(lambda n: dma),
        "c_r": each(lambda n: dma),
        "z_s": each(lambda n: dma((8,))),
        "z_r": each(lambda n: dma((8,))),
        "f_s": each(lambda n: dma((4,))),
        "f_r": each(lambda n: dma((4,))),
        "l_s": dma((4,)),
        "l_r": dma((4,)),
    }


class Refs:
    pass


def kernel(spec, th, sh, wt_hbm, ws_hbm, lab_hbm, loss_out, hg, hid_out, *scratch):
    m = Refs()
    scratch = list(scratch)
    for name, shape in spec.items():
        if isinstance(shape, list):
            setattr(m, name, [scratch.pop(0) for _ in shape])
        else:
            setattr(m, name, scratch.pop(0))
    tb = m.packed.shape[0]
    vb = m.wt.shape[1]
    s = lax.axis_index("section")
    z = lax.axis_index("vocab")
    x = lax.axis_index("dp")
    y, c = lax.div(s, 2), lax.rem(s, 2)
    right, left, opp = lax.rem(x + 1, 4), lax.rem(x + 3, 4), lax.rem(x + 2, 4)
    diagonal = x == y
    crossed = jnp.logical_not(diagonal)
    offset = (s * 8 + z) * vb
    starts = [sum(PARTS[:k]) for k in range(len(PARTS))]
    pending = []

    def dev(section=s, vocab=z, dp=x):
        return {"section": section, "vocab": vocab, "dp": dp}

    def remote(src, dst, ssem, rsem, to):
        return pltpu.make_async_remote_copy(
            src_ref=src, dst_ref=dst, send_sem=ssem, recv_sem=rsem,
            device_id=to, device_id_type=MESH,
        )

    def send(src, dst, ssem, rsem, to, cond=None):
        copy = remote(src, dst, ssem, rsem, to)
        if cond is None:
            copy.start()
        else:
            pl.when(cond)(copy.start)
        pending.append((cond, copy))

    def arrived(dst, ssem, rsem):
        remote(dst, dst, ssem, rsem, dev(dp=right)).wait_recv()

    other = dev(section=s + 1 - 2 * c)

    local = [
        pltpu.make_async_copy(th, m.turned.at[0:64], m.in_sem.at[0]),
        pltpu.make_async_copy(sh, m.turned.at[64:96], m.in_sem.at[1]),
        pltpu.make_async_copy(lab_hbm, m.lab, m.in_sem.at[2]),
        pltpu.make_async_copy(wt_hbm, m.wt, m.in_sem.at[3]),
        pltpu.make_async_copy(ws_hbm, m.ws, m.in_sem.at[4]),
    ]
    for copy in local:
        copy.start()

    barrier = pltpu.get_barrier_semaphore()

    def greet(to, unless=None):
        signal = functools.partial(
            pl.semaphore_signal, barrier, inc=1, device_id=to, device_id_type=MESH
        )
        if unless is None:
            signal()
        else:
            pl.when(jnp.logical_not(unless))(signal)

    def last_to(k):
        return dev(section=2 * x + c, dp=k), jnp.logical_and(diagonal, x == k)

    for k in range(1, 8):
        greet(dev(vocab=lax.rem(z + k, 8)))
    for k in range(1, 4):
        greet(dev(section=2 * x + c, dp=lax.rem(x + k, 4)))
    for k in range(4):
        greet(dev(section=2 * k + c, dp=y), diagonal)
    for k in range(1, 4):
        greet(dev(dp=lax.rem(x + k, 4)))
    for k in range(1, 8):
        greet(dev(section=lax.rem(s + k, 8)))

    for copy in local[:3]:
        copy.wait()
    m.turned[96:128, :] = jnp.zeros((32, tb), BF16)
    m.packed[...] = mm_nt(
        ones_where(iota((tb, tb), 0) == iota((tb, tb), 1)), m.turned[...]
    ).astype(BF16)
    pl.semaphore_wait(barrier, 20 + 4 * crossed.astype(I32))

    def hidden_first(p):
        rows = pl.ds(starts[p], PARTS[p])
        send(m.packed.at[rows], m.raw[p].at[z], m.h_s[p], m.h_r[p], dev(section=2 * x + c, dp=y), crossed)

        @pl.when(diagonal)
        def _():
            m.raw[p][z] = m.packed[rows, :]

    def hidden_z(p):
        ref = m.raw[p].at[z]

        @pl.when(crossed)
        def _():
            arrived(ref, m.h_s[p], m.h_r[p])

        for k in (4, 3, 5, 2, 6, 1, 7):
            send(ref, ref, m.r_s[p].at[k], m.r_r[p].at[z], dev(vocab=lax.rem(z + k, 8)))

    picks = []

    def hid_ref(p, core, yy):
        n = PARTS[p]
        return m.hid[p].at[core, pl.ds(pl.multiple_of(yy * n, n), n)]

    def hidden_y(p):
        for k in (1, 7, 2, 6, 3, 5, 4):
            frm = lax.rem(z + k, 8)
            arrived(m.raw[p].at[frm], m.r_s[p].at[k], m.r_r[p].at[frm])
        ref = hid_ref(p, c, y)
        for g in range(2):
            total = None
            for k in range(4):
                term = mm(m.raw[p][4 * g + k], picks[k])
                total = term if total is None else total + term
            ref[:, g * 256:(g + 1) * 256] = total[:, 0:256].astype(BF16)
            ref[:, 512 + g * 128:512 + (g + 1) * 128] = total[:, 256:384].astype(BF16)
        for k in (2, 1, 3):
            to = lax.rem(y + k, 4)
            send(ref, ref, m.u_s[p].at[k], m.u_r[p].at[y], dev(section=2 * to + c))
        send(ref, ref, m.w_s[p].at[y], m.w_r[p].at[y], other)

    def hidden_swap(p):
        for k in (1, 3, 2):
            frm = lax.rem(y + k, 4)
            ref = hid_ref(p, c, frm)
            arrived(ref, m.u_s[p].at[k], m.u_r[p].at[frm])
            send(ref, ref, m.w_s[p].at[frm], m.w_r[p].at[frm], other)

    def decode(p, slot, rows):
        if slot in (1, 4):
            level = m.qrecv[p][slot + 1, rows, vb:vb + 128][:, 64:65]
        else:
            level = m.qrecv[p][slot, rows, vb:vb + 128][:, 0:1]
        step = jnp.exp2(jnp.broadcast_to(level.astype(F32), (16, 128)) * 0.25 - TOP)
        return jnp.concatenate(
            [m.qrecv[p][slot, rows, i:i + 128].astype(F32) * step for i in range(0, vb, 128)],
            axis=1,
        )

    def word_refs(p, slot):
        lanes = slice(0, vb if slot in (1, 4) else vb + 128)
        return m.qsend[p].at[slot, :, lanes], m.qrecv[p].at[slot, :, lanes]

    def encode(p, slot, src, xp, dp, add=None):
        n = PARTS[p]

        def body(r, carry):
            rows = pl.ds(pl.multiple_of(r * 16, 16), 16)
            v = src[pl.ds(pl.multiple_of(xp * n + r * 16, 16), 16), :]
            if add is not None:
                v = v + decode(p, add, rows)
            top = jnp.maximum(jnp.max(jnp.abs(v), axis=1, keepdims=True), 1e-30)
            level = jnp.broadcast_to(jnp.ceil(jnp.log2(top) * 4.0), (16, 128))
            scale = jnp.exp2(TOP - level * 0.25)
            for i in range(0, vb, 128):
                q = jnp.round(v[:, i:i + 128] * scale).astype(I32)
                m.qsend[p][slot, rows, i:i + 128] = q.astype(I16)
            if slot in (1, 4):
                m.level[p][slot // 4, rows, :] = level
            else:
                if slot in (2, 5):
                    beside = m.level[p][slot // 5, rows, :]
                    level = jnp.where(iota((16, 128), 1) < 64, level, beside)
                m.qsend[p][slot, rows, vb:vb + 128] = level.astype(I32).astype(I16)
            return carry

        lax.fori_loop(0, n // 16, body, 0, unroll=True)
        src_words, dst_words = word_refs(p, slot)
        send(src_words, dst_words, m.q_s[p].at[slot], m.q_r[p].at[slot], dev(dp=dp))

    def landed(p, slot):
        arrived(word_refs(p, slot)[1], m.q_s[p].at[slot], m.q_r[p].at[slot])

    def logits(p):
        for k in range(4):
            arrived(hid_ref(p, 1 - c, k), m.w_s[p].at[k], m.w_r[p].at[k])

        def product(out, weights, lanes, depth):
            def body(i, carry):
                cols = pl.ds(pl.multiple_of(i * 256, 256), 256)
                out[:, cols] = mm(m.hid[p][0, :, lanes], weights[0:depth, cols]) + mm(
                    m.hid[p][1, :, lanes], weights[depth:2 * depth, cols]
                )
                return carry
            lax.fori_loop(0, vb // 256, body, 0)

        product(m.part_t[p], m.wt, slice(0, 512), 512)
        encode(p, 0, m.part_t[p], opp, right)
        product(m.part_s[p], m.ws, slice(512, 768), 256)
        encode(p, 3, m.part_s[p], opp, left)
        encode(p, 1, m.part_s[p], right, right)
        encode(p, 4, m.part_t[p], left, left)

    def fold(p):
        landed(p, 0)
        encode(p, 2, m.part_t[p], right, right, add=0)
        landed(p, 3)
        encode(p, 5, m.part_s[p], left, left, add=3)

    def row_span(p, r):
        n = PARTS[p]
        rows = pl.ds(pl.multiple_of(r * 16, 16), 16)
        own = pl.ds(pl.multiple_of(x * n + r * 16, 16), 16)
        toks = pl.ds(pl.multiple_of(starts[p] + r * 16, 16), 16)
        hit = offset + iota((16, vb), 1) == m.lab_col[toks, 0:1].astype(I32)
        return rows, own, hit

    def total_logits(p):
        for slot in (4, 1, 2, 5):
            landed(p, slot)
        m.stat[p][...] = jnp.ones((128, 128), F32)

        def body(r, carry):
            rows, own, hit = row_span(p, r)
            lt, ls = m.part_t[p][own, :], m.part_s[p][own, :]
            lt = lt + decode(p, 4, rows) + decode(p, 2, rows)
            ls = ls + decode(p, 1, rows) + decode(p, 5, rows)
            m.part_t[p][own, :] = lt
            m.part_s[p][own, :] = ls
            mt = jnp.max(lt, axis=1, keepdims=True)
            ms = jnp.max(ls, axis=1, keepdims=True)
            et = jnp.exp(lt - mt)
            es = jnp.exp(ls - ms)
            values = (
                mt,
                jnp.sum(et, axis=1, keepdims=True),
                jnp.sum(et * (lt - ls), axis=1, keepdims=True),
                ms,
                jnp.sum(es, axis=1, keepdims=True),
                jnp.sum(jnp.where(hit, ls, 0.0), axis=1, keepdims=True),
            )
            lane = iota((16, 128), 1)
            out = jnp.ones((16, 128), F32)
            for i, value in enumerate(values):
                out = jnp.where(lane == i, value, out)
            m.stat[p][rows, :] = out
            return carry

        lax.fori_loop(0, PARTS[p] // 16, body, 0, unroll=True)
        m.stat_z[p][z] = m.stat[p][...].T[0:8, :]
        ref = m.stat_z[p].at[z]
        for k in (4, 3, 5, 2, 6, 1, 7):
            send(ref, ref, m.sz_s[p].at[k], m.sz_r[p].at[z], dev(vocab=lax.rem(z + k, 8)))

    def merge(ref):
        tops_t = [ref[i, 0:1, :] for i in range(8)]
        tops_s = [ref[i, 3:4, :] for i in range(8)]
        mt = functools.reduce(jnp.maximum, tops_t)
        ms = functools.reduce(jnp.maximum, tops_s)
        zt = at = zs = sy = 0.0
        for i in range(8):
            wt_i = jnp.exp(tops_t[i] - mt)
            ws_i = jnp.exp(tops_s[i] - ms)
            zt = zt + ref[i, 1:2, :] * wt_i
            at = at + ref[i, 2:3, :] * wt_i
            zs = zs + ref[i, 4:5, :] * ws_i
            sy = sy + ref[i, 5:6, :]
        return mt, zt, at, ms, zs, sy

    def stats_z(p):
        for k in range(1, 8):
            frm = lax.rem(z + k, 8)
            arrived(m.stat_z[p].at[frm], m.sz_s[p].at[k], m.sz_r[p].at[frm])
        row = iota((8, 128), 0)
        out = jnp.ones((8, 128), F32)
        for i, value in enumerate(merge(m.stat_z[p])):
            out = jnp.where(row == i, value, out)
        m.stat_s[p][s] = out
        ref = m.stat_s[p].at[s]
        for k in (4, 3, 5, 2, 6, 1, 7):
            send(ref, ref, m.ss_s[p].at[k], m.ss_r[p].at[s], dev(section=lax.rem(s + k, 8)))

    losses = []

    def gradient(p):
        n = PARTS[p]
        for k in range(1, 8):
            frm = lax.rem(s + k, 8)
            arrived(m.stat_s[p].at[frm], m.ss_s[p].at[k], m.ss_r[p].at[frm])
        mt, zt, at, ms, zs, sy = merge(m.stat_s[p])
        lse_t = mt + jnp.log(zt)
        lse_s = ms + jnp.log(zs)
        per_token = at / zt - lse_t + lse_s - label_weight * (sy - lse_s)
        per_token = jnp.where(iota((1, 128), 1) < n, per_token, 0.0)
        losses.append(jnp.sum(per_token, axis=1, keepdims=True))
        row = iota((128, 128), 0)
        m.lse[p][...] = jnp.where(row == 0, lse_t, lse_s).T

        def body(r, carry):
            rows, own, hit = row_span(p, r)
            pt = jnp.exp(m.part_t[p][own, :] - m.lse[p][rows, 0:1])
            ps = jnp.exp(m.part_s[p][own, :] - m.lse[p][rows, 1:2])
            value = (1.0 + label_weight) * ps - pt - jnp.where(hit, label_weight, 0.0)
            m.grad[p][own, :] = value.astype(BF16)
            return carry

        lax.fori_loop(0, n // 16, body, 0, unroll=True)
        ref = grad_ref(p, x)
        for k in (2, 1, 3):
            send(ref, ref, m.g_s[p].at[k], m.g_r[p].at[x], dev(dp=lax.rem(x + k, 4)))

    def grad_ref(p, xp):
        n = PARTS[p]
        return m.grad[p].at[pl.ds(pl.multiple_of(xp * n, n), n)]

    def hidden_back(p):
        for k in (1, 3, 2):
            frm = lax.rem(x + k, 4)
            arrived(grad_ref(p, frm), m.g_s[p].at[k], m.g_r[p].at[frm])
        theirs = pl.ds(pl.multiple_of((1 - c) * 256, 256), 256)
        ours = pl.ds(pl.multiple_of(c * 256, 256), 256)
        m.csend[p][...] = mm_nt(m.ws[theirs, :], m.grad[p][...]).astype(BF16)
        send(m.csend[p], m.crecv[p], m.c_s[p], m.c_r[p], other)
        m.hown[p][...] = mm_nt(m.ws[ours, :], m.grad[p][...])

    def slice_ref(ref, zz):
        return ref.at[pl.ds(pl.multiple_of(zz * 32, 32), 32)]

    def hidden_spread(p):
        arrived(m.crecv[p], m.c_s[p], m.c_r[p])
        total = m.hown[p][...] + m.crecv[p][...].astype(F32)
        m.hown[p][...] = total
        m.zsend[p][...] = total.astype(BF16)
        for k in (4, 3, 5, 2, 6, 1, 7):
            to = lax.rem(z + k, 8)
            send(slice_ref(m.zsend[p], to), m.zrecv[p].at[z], m.z_s[p].at[k], m.z_r[p].at[z],
                 dev(vocab=to))

    def hidden_owner(p):
        total = slice_ref(m.hown[p], z)[...]
        for k in range(1, 8):
            frm = lax.rem(z + k, 8)
            arrived(m.zrecv[p].at[frm], m.z_s[p].at[k], m.z_r[p].at[frm])
            total = total + m.zrecv[p][frm].astype(F32)
        m.fsend[p][...] = total.astype(BF16)
        for k in range(4):
            to, here = last_to(k)
            send(m.fsend[p], m.frecv[p].at[y], m.f_s[p].at[k], m.f_r[p].at[y], to,
                 jnp.logical_not(here))

        @pl.when(diagonal)
        def _():
            m.frecv[p][y] = m.fsend[p][...]

    def hidden_final(p):
        n = PARTS[p]
        for k in range(4):
            @pl.when(jnp.logical_not(jnp.logical_and(diagonal, y == k)))
            def _(k=k):
                arrived(m.frecv[p].at[k], m.f_s[p].at[k], m.f_r[p].at[k])
        total = m.frecv[p][0].astype(F32)
        for k in range(1, 4):
            total = total + m.frecv[p][k].astype(F32)
        lane, token = iota((4 * n, tb), 0), iota((4 * n, tb), 1) - starts[p]
        inside = jnp.logical_and(token >= 0, token < n)
        place = ones_where(jnp.logical_and(inside, lane == x * n + token))
        return mm(total.astype(BF16), place)

    def turn_student(p):
        eye = ones_where(iota((128, 128), 0) == iota((128, 128), 1))
        for u in range(4):
            lanes = slice(512 + (u % 2) * 128, 640 + (u % 2) * 128)
            flat = mm_nt(eye, m.hid[p][u // 2, :, lanes])
            m.hst[p][u * 128:(u + 1) * 128, :] = flat.astype(BF16)

    def head_terms():
        def body(i, carry):
            cols = pl.ds(pl.multiple_of(i * 256, 256), 256)
            total = None
            for p in range(len(PARTS)):
                term = mm(m.hst[p][...], m.grad[p][:, cols])
                total = term if total is None else total + term
            hg[:, cols] = total
            return carry
        lax.fori_loop(0, vb // 256, body, 0)

    def prepare():
        m.wide[...] = jnp.zeros_like(m.wide)
        m.wide[0:1, 0:tb] = m.lab[...].astype(F32)
        m.lab_col[...] = m.wide[...].T
        for k in range(4):
            rows, lanes = iota((128, 384), 0), iota((128, 384), 1)
            place = jnp.where(rows < 64, rows + 64 * k, rows - 64 + 256 + 32 * k)
            picks.append(ones_where(jnp.logical_and(lanes == place, rows < 96)))
        local[3].wait()
        local[4].wait()

    def loss_send():
        m.loss[x] = jnp.broadcast_to(functools.reduce(jnp.add, losses), (8, 128))
        for k in range(1, 4):
            send(m.loss.at[x], m.loss.at[x], m.l_s.at[k], m.l_r.at[x], dev(dp=lax.rem(x + k, 4)))

    def loss_sum():
        for k in range(1, 4):
            frm = lax.rem(x + k, 4)
            arrived(m.loss.at[frm], m.l_s.at[k], m.l_r.at[frm])
        loss = functools.reduce(jnp.add, [m.loss[k, 0:1, 0:1] for k in range(4)])
        loss_out[0, 0] = jnp.sum(loss) / (4.0 * tb)

    def finish():
        for cond, copy in pending:
            if cond is None:
                copy.wait_send()
            else:
                pl.when(cond)(copy.wait_send)
        out = functools.reduce(jnp.add, [hidden_final(p) for p in range(len(PARTS))])
        hid_out[...] = out.astype(BF16)

    per_part = {
        "F": hidden_first, "Z": hidden_z, "Y": hidden_y, "W": hidden_swap, "L": logits,
        "U": turn_student, "O": fold, "T": total_logits, "S": stats_z, "G": gradient,
        "B": hidden_back, "P": hidden_spread, "N": hidden_owner,
    }
    once = {"I": prepare, "X": loss_send, "X2": loss_sum, "H": head_terms, "E": finish}
    for step in ORDER:
        if step in once:
            once[step]()
        else:
            per_part[step[0]](int(step[1]))


def per_device(teacher_hidden, student_hidden, teacher_head, student_head, labels):
    tb = teacher_hidden.shape[0]
    kt, vb = teacher_head.shape
    ks = student_head.shape[0]
    spec = buffers(tb, kt, ks, vb)
    flat = []
    for shape in spec.values():
        flat.extend(shape if isinstance(shape, list) else [shape])
    hbm = pl.BlockSpec(memory_space=pltpu.HBM)
    vmem = pl.BlockSpec(memory_space=pltpu.VMEM)
    loss, head_grad, hidden_grad = pl.pallas_call(
        functools.partial(kernel, spec),
        out_shape=(
            jax.ShapeDtypeStruct((1, 1), F32),
            pltpu.VMEM((ks, vb), F32),
            pltpu.VMEM((32, tb), BF16),
        ),
        in_specs=[hbm] * 5,
        out_specs=(pl.BlockSpec(memory_space=pltpu.SMEM), vmem, vmem),
        scratch_shapes=flat,
        compiler_params=pltpu.CompilerParams(
            collective_id=0, has_side_effects=True, vmem_limit_bytes=58 * 1024 * 1024
        ),
    )(teacher_hidden.T, student_hidden.T, teacher_head, student_head, labels.reshape(1, tb))
    return (loss.reshape(()), head_grad, hidden_grad.T)


def solution(mesh):
    spec = P("dp", ("section", "vocab"))
    return jax.shard_map(
        per_device,
        mesh=mesh,
        in_specs=(spec, spec, spec, spec, P("dp")),
        out_specs=(P(), spec, spec),
        check_vma=False,
    )
```

time: 692 us -> 87.3 us (0.13)
  waiting for transfers between devices: 337 us -> 0 us
  blocking collectives: 314 us -> 0 us
  Pallas kernels: 0 us -> 82.8 us
  matrix products: 16.9 us -> 0 us
  between operations: 15.6 us -> 2.33 us
    reduce_scatter x2 -> x0, waiting for transfers between devices: 171 us -> none  [the longest x1 124 us: per_device(): lax.psum_scatter(back_terms, ('section', 'vocab'), scatter_dimension=1, t...]
    all_gather x3 -> x0, waiting for transfers between devices: 164 us -> none  [the longest x1 84.9 us: per_device(): lax.all_gather(teacher_head, 'dp', axis=0, tiled=True)]
    psum x2 -> x0, blocking collectives: 132 us -> none  [the longest x1 124 us: per_device(): lax.psum((local_zt * shift_t, local_at * shift_t, local_zs * shift_s, loc...]
    pmax x1 -> x0, blocking collectives: 129 us -> none  [per_device(): top_t, top_s = lax.pmax((local_mt, local_ms), ('section', 'vocab'))]
    pallas_call x0 -> x1, Pallas kernels: none -> 82.8 us  [per_device(): pl.pallas_call(functools.partial(kernel, spec), out_shape=(jax.ShapeDtype...]
    all_gather x1 -> x0, blocking collectives: 52.6 us -> none  [per_device(): lax.all_gather(student_hidden, ('section', 'vocab'), axis=1, tiled=True)]
    dot_general x4 -> x0, matrix products: 16.9 us -> none  [the longest x1 5.67 us: per_device(): jnp.dot(wide_t, lax.all_gather(teacher_head, 'dp', axis=0, tiled=True), p...]
  transfers between devices with their start and end apart: 5 -> 0, of which waited for: 5 -> 0; matrix products, arithmetic and copies ran while one was open for 1% -> 0% of each run, Pallas kernels for 0% -> 0%
where the time goes in v2:
time: 87.3 us; the launch traced here: 87 us
  Pallas kernels  82.8 us (95%)
  between operations  2.33 us (3%)
  local copies, waits for them, and re-layouts  1.93 us (2%)
    pallas_call x1, Pallas kernels, per_device(): pl.pallas_call(functools.partial(kernel, spec), out_shape=(jax.ShapeDtype...  82.8 us
    unnamed x2, local copies, waits for them, and re-layouts  1.93 us

profile of v2, /device:TPU:4, one launch (start us, length us, event | category | flops | bytes accessed | tf_op | source)
XLA Modules:
  0.0 87.0 jit_solution(5313250945955027048)
XLA Ops:
  0.6 82.8 %shard_map.76 = (f32[1,1]{1,0:T(1,128)}, f32[512,1024]{1,0:T(8,128)S(1)}, bf16[32,160]{1,0:T(8,128)(2,1)S(1)}) custom-call(bf16[64,160]{1,0:T(8,128)(2,1)} %bitcast.6, bf16[32,160]{1,0:T(8,128)(2,1)} %bitcast.7, bf16[1024,1024]{1,0:T(8,128)(2,1)} %wt_hbm.1, bf16[512,1024]{1,0:T(8,128)(2,1)} %ws_hbm.1, s32[1,160]{1,0:T(1,128)} %bitcast.8), custom_call_target="tpu_custom_call" | custom-call | tf_op jit(solution)/shard_map/pallas_call | solution.py:542
  83.4 1.3 %copy.11 = f32[512,1024]{1,0:T(8,128)} copy(f32[512,1024]{1,0:T(8,128)S(1)} %get-tuple-element.10) | data formatting | bytes 4194304
  84.7 0.6 copy.12

commit v3 on v2

--- a/solution.py
+++ b/solution.py
@@ -12,7 +12,7 @@
 TOP = 14.99
 PARTS = (48, 64, 48)
 ORDER = (
-    "F2", "F1", "I", "Z2", "F0", "Z1", "Y2", "Y1", "W2", "Z0", "L2", "W1", "Y0", "U2",
+    "F", "I", "Z2", "Z1", "Y2", "Y1", "W2", "Z0", "L2", "W1", "Y0", "U2",
     "O2", "L1", "T2", "W0", "O1", "L0", "U1", "T1", "S2", "O0", "S1", "G2", "T0", "G1",
     "U0", "S0", "B2", "G0", "P2", "B1", "P1", "B0", "P0", "N1", "X", "N2", "H", "X2",
     "N0", "E",
@@ -49,7 +49,7 @@
         "packed": vmem((tb, 128), BF16),
         "wide": vmem((128, 256), F32),
         "lab_col": vmem((256, 128), F32),
-        "raw": each(lambda n: vmem((8, n, 128), BF16)),
+        "raw": vmem((8, tb, 128), BF16),
         "hid": each(lambda n: vmem((2, 4 * n, 768), BF16)),
         "hst": each(lambda n: vmem((ks, 4 * n), BF16)),
         "part_t": each(lambda n: vmem((4 * n, vb), F32)),
@@ -71,8 +71,8 @@
         "frecv": each(lambda n: vmem((4, 32, 4 * n), BF16)),
         "loss": vmem((4, 8, 128), F32),
         "in_sem": dma((5,)),
-        "h_s": each(lambda n: dma),
-        "h_r": each(lambda n: dma),
+        "h_s": dma,
+        "h_r": dma,
         "r_s": each(lambda n: dma((8,))),
         "r_r": each(lambda n: dma((8,))),
         "u_s": each(lambda n: dma((4,))),
@@ -121,7 +121,7 @@
     crossed = jnp.logical_not(diagonal)
     offset = (s * 8 + z) * vb
     starts = [sum(PARTS[:k]) for k in range(len(PARTS))]
-    pending = []
+    pending, steps = [], []
 
     def dev(section=s, vocab=z, dp=x):
         return {"section": section, "vocab": vocab, "dp": dp}
@@ -138,7 +138,7 @@
             copy.start()
         else:
             pl.when(cond)(copy.start)
-        pending.append((cond, copy))
+        pending.append((len(steps), cond, copy))
 
     def arrived(dst, ssem, rsem):
         remote(dst, dst, ssem, rsem, dev(dp=right)).wait_recv()
@@ -188,21 +188,23 @@
     ).astype(BF16)
     pl.semaphore_wait(barrier, 20 + 4 * crossed.astype(I32))
 
-    def hidden_first(p):
-        rows = pl.ds(starts[p], PARTS[p])
-        send(m.packed.at[rows], m.raw[p].at[z], m.h_s[p], m.h_r[p], dev(section=2 * x + c, dp=y), crossed)
+    def hidden_first():
+        send(m.packed, m.raw.at[z], m.h_s, m.h_r, dev(section=2 * x + c, dp=y), crossed)
 
         @pl.when(diagonal)
         def _():
-            m.raw[p][z] = m.packed[rows, :]
+            m.raw[z] = m.packed[...]
+
+    def raw_ref(p, zz):
+        return m.raw.at[zz, pl.ds(starts[p], PARTS[p])]
 
     def hidden_z(p):
-        ref = m.raw[p].at[z]
-
-        @pl.when(crossed)
-        def _():
-            arrived(ref, m.h_s[p], m.h_r[p])
-
+        if not any(step[0] == "Z" for step in steps[:-1]):
+            @pl.when(crossed)
+            def _():
+                arrived(m.raw.at[z], m.h_s, m.h_r)
+
+        ref = raw_ref(p, z)
         for k in (4, 3, 5, 2, 6, 1, 7):
             send(ref, ref, m.r_s[p].at[k], m.r_r[p].at[z], dev(vocab=lax.rem(z + k, 8)))
 
@@ -215,12 +217,12 @@
     def hidden_y(p):
         for k in (1, 7, 2, 6, 3, 5, 4):
             frm = lax.rem(z + k, 8)
-            arrived(m.raw[p].at[frm], m.r_s[p].at[k], m.r_r[p].at[frm])
+            arrived(raw_ref(p, frm), m.r_s[p].at[k], m.r_r[p].at[frm])
         ref = hid_ref(p, c, y)
         for g in range(2):
             total = None
             for k in range(4):
-                term = mm(m.raw[p][4 * g + k], picks[k])
+                term = mm(raw_ref(p, 4 * g + k)[...], picks[k])
                 total = term if total is None else total + term
             ref[:, g * 256:(g + 1) * 256] = total[:, 0:256].astype(BF16)
             ref[:, 512 + g * 128:512 + (g + 1) * 128] = total[:, 256:384].astype(BF16)
@@ -507,22 +509,29 @@
         loss = functools.reduce(jnp.add, [m.loss[k, 0:1, 0:1] for k in range(4)])
         loss_out[0, 0] = jnp.sum(loss) / (4.0 * tb)
 
-    def finish():
-        for cond, copy in pending:
+    def settle(age):
+        while pending and len(steps) - pending[0][0] >= age:
+            _, cond, copy = pending.pop(0)
             if cond is None:
                 copy.wait_send()
             else:
                 pl.when(cond)(copy.wait_send)
+
+    def finish():
+        settle(0)
         out = functools.reduce(jnp.add, [hidden_final(p) for p in range(len(PARTS))])
         hid_out[...] = out.astype(BF16)
 
     per_part = {
-        "F": hidden_first, "Z": hidden_z, "Y": hidden_y, "W": hidden_swap, "L": logits,
+        "Z": hidden_z, "Y": hidden_y, "W": hidden_swap, "L": logits,
         "U": turn_student, "O": fold, "T": total_logits, "S": stats_z, "G": gradient,
         "B": hidden_back, "P": hidden_spread, "N": hidden_owner,
     }
-    once = {"I": prepare, "X": loss_send, "X2": loss_sum, "H": head_terms, "E": finish}
+    once = {"F": hidden_first, "I": prepare, "X": loss_send, "X2": loss_sum, "H": head_terms, "E": finish}
     for step in ORDER:
+        steps.append(step)
+        if step[0] in "SGBN":
+            settle(8)
         if step in once:
             once[step]()
         else:

time: 87.3 us -> 87.9 us (level)
  no operation moved by 1% of the time
where the time goes in v3:
time: 87.9 us; the launch traced here: 87.5 us
  Pallas kernels  83.3 us (95%)
  between operations  2.33 us (3%)
  local copies, waits for them, and re-layouts  1.93 us (2%)
    pallas_call x1, Pallas kernels, per_device(): pl.pallas_call(functools.partial(kernel, spec), out_shape=(jax.ShapeDtype...  83.3 us
    unnamed x2, local copies, waits for them, and re-layouts  1.93 us

profile of v3, /device:TPU:4, one launch (start us, length us, event | category | flops | bytes accessed | tf_op | source)
XLA Modules:
  0.0 87.5 jit_solution(2647724967192514141)
XLA Ops:
  0.6 83.3 %shard_map.76 = (f32[1,1]{1,0:T(1,128)}, f32[512,1024]{1,0:T(8,128)S(1)}, bf16[32,160]{1,0:T(8,128)(2,1)S(1)}) custom-call(bf16[64,160]{1,0:T(8,128)(2,1)} %bitcast.6, bf16[32,160]{1,0:T(8,128)(2,1)} %bitcast.7, bf16[1024,1024]{1,0:T(8,128)(2,1)} %wt_hbm.1, bf16[512,1024]{1,0:T(8,128)(2,1)} %ws_hbm.1, s32[1,160]{1,0:T(1,128)} %bitcast.8), custom_call_target="tpu_custom_call" | custom-call | tf_op jit(solution)/shard_map/pallas_call | solution.py:551
  83.9 1.3 %copy.11 = f32[512,1024]{1,0:T(8,128)} copy(f32[512,1024]{1,0:T(8,128)S(1)} %get-tuple-element.10) | data formatting | bytes 4194304
  85.2 0.6 copy.12
